TPU v7x, 512 devices: a whole 4x8x8 slice. The times are simulated.
512 devices in a mesh: lon: 32 (over z_hi, x, core), lat: 16 (over y, z_lo).
Axes of the slice: x: 4, y: 8, z: 8 (z_hi: 4, z_lo: 2; z = z_hi * 2 + z_lo), core: 2. Of those that a mesh axis runs over, the one named last changes fastest.
Arguments:
- fields: bfloat16 [96, 128, 8192], P(None, 'lat', 'lon'), may hold values from -6 to 6
- land_mask: int32 [128, 8192], P('lat', 'lon'), may hold values from 0 to 1, as said below
- dw_kernel: float32 [96, 7, 7], replicated, may hold values from -0.875 to 0.875
- gain: float32 [96], replicated, may hold values from 0.1 to 1.9
- w_in: bfloat16 [96, 192], replicated, may hold values from -0.625 to 0.625
- b_in: float32 [192], replicated, may hold values from -3 to 3
- w_out: bfloat16 [192, 96], replicated, may hold values from -0.4375 to 0.4375
- cotangent: bfloat16 [96, 128, 8192], P(None, 'lat', 'lon'), may hold values from -6 to 6
Outputs:
- output: bfloat16 [96, 128, 8192], P(None, 'lat', 'lon')
- input_grad: bfloat16 [96, 128, 8192], P(None, 'lat', 'lon')
- kernel_grad: float32 [96, 7, 7], replicated
- gain_grad: float32 [96], replicated
- w_in_grad: float32 [96, 192], replicated
- b_in_grad: float32 [192], replicated
- w_out_grad: float32 [192, 96], replicated
Inputs may be any that keep to these rules, and one draw needn't show every extreme that they name: `land_mask`: 1 marks a sea cell and 0 a land cell.
All inputs are finite; a program needn't handle non-finite values.
Results may differ from a plain program's by a relative error of at most 0.009.
Values may be sent and summed in bfloat16 or wider, within the bound.
No kernel may reach another device: no remote copies, remote signals or barrier semaphores. Data moves between devices by JAX's collectives and lax.ppermute only.
A program may use at most 192 MiB of HBM per device.

v0:
```python
import jax
import jax.numpy as jnp
from jax import lax
from jax.sharding import PartitionSpec as P


def from_partner(block, axis, stride):
    count = lax.axis_size(axis)
    route = []
    for low in range(count):
        high = low | 1 << stride
        if high != low and high < count:
            route += [(low, high), (high, low)]
    return lax.ppermute(block, axis, route)


def extended(shard, sides, width, wrap):
    for axis, dim in sides:
        size, length = (lax.axis_size(axis), shard.shape[dim])
        up = [(i, (i + 1) % size) for i in range(size if wrap else size - 1)]
        down = [(j, i) for i, j in up]
        last = lax.slice_in_dim(shard, length - width, length, axis=dim)
        first = lax.slice_in_dim(shard, 0, width, axis=dim)
        before = lax.ppermute(last, axis, up)
        after = lax.ppermute(first, axis, down)
        shard = jnp.concatenate([before, shard, after], axis=dim)
    return shard


def mirror_forward(values):
    steps_count = lax.axis_size("lon").bit_length() - 1
    for bit_pos in range(steps_count):
        values = from_partner(values, "lon", bit_pos)
    return values[:, ::-1, ::-1]


def mirror_backward(values):
    steps_count = lax.axis_size("lon").bit_length() - 1
    for bit_pos in range(steps_count):
        values = from_partner(values.astype(jnp.bfloat16), "lon", bit_pos).astype(values.dtype)
    return values[:, ::-1, ::-1]


def convolve(padded, kernel, tile_rows, tile_cols):
    summed = jnp.zeros((padded.shape[0], tile_rows, tile_cols), jnp.float32)
    for row_off in range(7):
        for col_off in range(7):
            window = padded[:, row_off : row_off + tile_rows, col_off : col_off + tile_cols].astype(
                jnp.float32
            )
            summed = summed + kernel[:, row_off, col_off][:, None, None] * window
    return summed


def spread_back(conv_grad, kernel):
    channels, tile_rows, tile_cols = conv_grad.shape
    bordered = jnp.pad(conv_grad, ((0, 0), (6, 6), (6, 6)))
    summed = jnp.zeros((channels, tile_rows + 6, tile_cols + 6), jnp.float32)
    for row_off in range(7):
        for col_off in range(7):
            window = bordered[
                :, 6 - row_off : 12 - row_off + tile_rows, 6 - col_off : 12 - col_off + tile_cols
            ]
            summed = summed + kernel[:, row_off, col_off][:, None, None] * window
    return summed


def kernel_terms(conv_grad, padded):
    channels, tile_rows, tile_cols = conv_grad.shape
    terms = []
    for row_off in range(7):
        for col_off in range(7):
            window = padded[:, row_off : row_off + tile_rows, col_off : col_off + tile_cols].astype(
                jnp.float32
            )
            terms.append(jnp.sum(conv_grad * window, axis=(1, 2)))
    return jnp.stack(terms, axis=1).reshape(channels, 7, 7)


def shards(fields, land_mask, dw_kernel, gain, w_in, b_in, w_out, cotangent):
    channels, tile_rows, tile_cols = fields.shape
    sea_mask = land_mask.astype(jnp.bfloat16)[None]
    masked = fields * sea_mask
    back_sea = cotangent * sea_mask
    lat_pos = lax.axis_index("lat")
    is_bottom = lat_pos == 0
    is_top = lat_pos == lax.axis_size("lat") - 1
    padded = extended(masked, (("lon", 2), ("lat", 1)), 3, True)
    folded = mirror_forward(padded[:, tile_rows : tile_rows + 3, :])
    south = jnp.where(is_bottom, jnp.zeros_like(padded[:, :3, :]), padded[:, :3, :])
    north = jnp.where(is_top, folded, padded[:, tile_rows + 3 :, :])
    padded = jnp.concatenate([south, padded[:, 3 : tile_rows + 3, :], north], axis=1)
    conv_out = convolve(padded, dw_kernel, tile_rows, tile_cols)
    centred = conv_out - jnp.mean(conv_out, axis=0, keepdims=True)
    inv_std = lax.rsqrt(jnp.mean(centred * centred, axis=0, keepdims=True) + 1e-06)
    normed = centred * inv_std
    scaled = (normed * gain[:, None, None]).astype(jnp.bfloat16)
    hidden_pre = (
        jnp.einsum("ch,cxy->hxy", w_in, scaled, preferred_element_type=jnp.float32)
        + b_in[:, None, None]
    )
    activated, gelu_pull = jax.vjp(jax.nn.gelu, hidden_pre)
    activated = activated.astype(jnp.bfloat16)
    mixed = jnp.einsum("hc,hxy->cxy", w_out, activated, preferred_element_type=jnp.float32)
    centre = padded[:, 3 : tile_rows + 3, 3 : tile_cols + 3].astype(jnp.float32)
    output = (sea_mask * (centre + mixed)).astype(jnp.bfloat16)
    w_out_part = jnp.einsum("hxy,cxy->hc", activated, back_sea, preferred_element_type=jnp.float32)
    act_grad = jnp.einsum("hc,cxy->hxy", w_out, back_sea, preferred_element_type=jnp.float32)
    pre_grad = gelu_pull(act_grad)[0].astype(jnp.bfloat16)
    output, w_out_part, pre_grad, scaled, normed, inv_std = (
        output,
        w_out_part,
        pre_grad,
        scaled,
        normed,
        inv_std,
    )
    b_part = jnp.sum(pre_grad.astype(jnp.float32), axis=(1, 2))
    w_in_part = jnp.einsum("cxy,hxy->ch", scaled, pre_grad, preferred_element_type=jnp.float32)
    scaled_grad = jnp.einsum("ch,hxy->cxy", w_in, pre_grad, preferred_element_type=jnp.float32)
    gain_part = jnp.sum(scaled_grad * normed, axis=(1, 2))
    norm_grad = scaled_grad * gain[:, None, None]
    conv_grad = inv_std * (
        norm_grad
        - jnp.mean(norm_grad, axis=0, keepdims=True)
        - normed * jnp.mean(norm_grad * normed, axis=0, keepdims=True)
    )
    kernel_part = kernel_terms(conv_grad, padded)
    ext_grad = spread_back(conv_grad, dw_kernel)
    kernel_part, gain_part, w_in_part, b_part, ext_grad = (
        kernel_part,
        gain_part,
        w_in_part,
        b_part,
        ext_grad,
    )
    kernel_sum, gain_sum, w_in_sum, b_sum, w_out_sum = lax.psum(
        (kernel_part, gain_part, w_in_part, b_part, w_out_part), ("lon", "lat")
    )
    returned = mirror_backward(ext_grad[:, tile_rows + 3 :, :])
    ext_grad = ext_grad.at[:, tile_rows : tile_rows + 3, :].add(
        jnp.where(is_top, returned, jnp.zeros_like(returned))
    )
    rims = jnp.concatenate([ext_grad[:, :3, :], ext_grad[:, tile_rows + 3 :, :]], axis=1)
    got_rows = extended(rims.astype(jnp.bfloat16), (("lat", 1),), 3, False).astype(rims.dtype)
    inner = ext_grad[:, 3 : tile_rows + 3, :]
    inner = inner.at[:, :3, :].add(got_rows[:, :3, :])
    inner = inner.at[:, tile_rows - 3 :, :].add(got_rows[:, 9:, :])
    sides = jnp.concatenate([inner[:, :, :3], inner[:, :, tile_cols + 3 :]], axis=2)
    sides = jnp.transpose(sides, (2, 0, 1)).reshape(6, channels * tile_rows)
    got_cols = extended(sides, (("lon", 0),), 3, True)
    from_left = jnp.transpose(got_cols[:3].reshape(3, channels, tile_rows), (1, 2, 0))
    from_right = jnp.transpose(got_cols[9:].reshape(3, channels, tile_rows), (1, 2, 0))
    core = inner[:, :, 3 : tile_cols + 3]
    core = core.at[:, :, :3].add(from_left)
    core = core.at[:, :, tile_cols - 3 :].add(from_right)
    input_grad = (sea_mask * (core + back_sea.astype(jnp.float32))).astype(jnp.bfloat16)
    scale_factor = float(tile_rows * tile_cols * lax.axis_size("lat") * lax.axis_size("lon")) ** (
        -0.5
    )
    return (
        output,
        input_grad,
        kernel_sum * scale_factor,
        gain_sum * scale_factor,
        w_in_sum * scale_factor,
        b_sum * scale_factor,
        w_out_sum * scale_factor,
    )


def solution(mesh):
    return jax.shard_map(
        shards,
        mesh=mesh,
        in_specs=(
            P(None, "lat", "lon"),
            P("lat", "lon"),
            P(),
            P(),
            P(),
            P(),
            P(),
            P(None, "lat", "lon"),
        ),
        out_specs=(P(None, "lat", "lon"), P(None, "lat", "lon"), P(), P(), P(), P(), P()),
        check_vma=False,
    )
```

profile of v0, /device:TPU:7, one launch (start us, length us, event | category | flops | bytes accessed | tf_op | source)
XLA Modules:
  0.0 450.5 jit_solution(8596428200641927452)
XLA Ops:
  7.9 1.1 copy_multiply_fusion.1
  9.1 6.3 %collective-permute-start = (bf16[96,8,3]{2,0,1:T(8,128)(2,1)S(1)}, bf16[96,8,3]{2,0,1:T(8,128)(2,1)S(1)}, u32[]{:S(2)}, u32[]{:S(2)}) collective-permute-start(bf16[96,8,3]{2,0,1:T(8,128)(2,1)S(1)} %get-tuple-element.168), channel_id=1, source_target_pairs={{0,16},{16,32},{32,48},{48,64},{64,80},{80,96},{96,112},{112,128},... | collective-permute-start | bytes 13832 | tf_op jit(solution)/shard_map/ppermute | solution.py:24
  15.4 1.9 collective-permute-start.1
  18.0 9.6 %collective-permute-done.1 = bf16[96,8,3]{2,0,1:T(8,128)(2,1)S(1)} collective-permute-done((bf16[96,8,3]{2,0,1:T(8,128)(2,1)S(1)}, bf16[96,8,3]{2,0,1:T(8,128)(2,1)S(1)}, u32[]{:S(2)}, u32[]{:S(2)}) %collective-permute-start.1) | collective-permute-done | bytes 4640 | tf_op jit(solution)/shard_map/ppermute | solution.py:25
  27.9 1.9 collective-permute-start.3
  29.8 1.4 collective-permute-done.3
  31.3 1.9 collective-permute-start.4
  33.4 6.7 %collective-permute-done.4 = bf16[96,3,262]{2,0,1:T(8,128)(2,1)S(1)} collective-permute-done((bf16[96,3,262]{2,0,1:T(8,128)(2,1)S(1)}, bf16[96,3,262]{2,0,1:T(8,128)(2,1)S(1)}, u32[]{:S(2)}, u32[]{:S(2)}) %collective-permute-start.4) | collective-permute-done | bytes 150944 | tf_op jit(solution)/shard_map/ppermute | solution.py:14
  40.1 4.1 collective-permute-start.5
  44.4 1.9 collective-permute-start.2
  46.3 3.1 collective-permute-done.5
  49.4 8.1 %collective-permute-start.6 = (bf16[96,3,262]{2,0,1:T(8,128)(2,1)S(1)}, bf16[96,3,262]{2,0,1:T(8,128)(2,1)S(1)}, u32[]{:S(2)}, u32[]{:S(2)}) collective-permute-start(bf16[96,3,262]{2,0,1:T(8,128)(2,1)S(1)} %collective-permute-done.5), channel_id=1, source_target_pairs={{0,128},{128,0},{16,144},{144,16},{32,160},{160,32},{48,176},{176,... | collective-permute-start | bytes 452744 | tf_op jit(solution)/shard_map/ppermute | solution.py:14
  58.1 5.2 %collective-permute-start.8 = (bf16[96,3,262]{2,0,1:T(8,128)(2,1)S(1)}, bf16[96,3,262]{2,0,1:T(8,128)(2,1)S(1)}, u32[]{:S(2)}, u32[]{:S(2)}) collective-permute-start(bf16[96,3,262]{2,0,1:T(8,128)(2,1)S(1)} %get-tuple-element.166), channel_id=1, source_target_pairs={{1,0},{2,1},{3,2},{4,3},{5,4},{6,5},{7,6},{8,7},{9,8},{10,9},{11,1... | collective-permute-start | bytes 452744 | tf_op jit(solution)/shard_map/ppermute | solution.py:25
  63.3 4.0 collective-permute-done.6
  67.3 5.6 %collective-permute-start.7 = (bf16[96,3,262]{2,0,1:T(8,128)(2,1)S(1)}, bf16[96,3,262]{2,0,1:T(8,128)(2,1)S(1)}, u32[]{:S(2)}, u32[]{:S(2)}) collective-permute-start(bf16[96,3,262]{2,0,1:T(8,128)(2,1)S(1)} %collective-permute-done.6), channel_id=1, source_target_pairs={{0,256},{256,0},{16,272},{272,16},{32,288},{288,32},{48,304},{304,... | collective-permute-start | bytes 452744 | tf_op jit(solution)/shard_map/ppermute | solution.py:14
  73.0 9.9 %collective-permute-done.7 = bf16[96,3,262]{2,0,1:T(8,128)(2,1)S(1)} collective-permute-done((bf16[96,3,262]{2,0,1:T(8,128)(2,1)S(1)}, bf16[96,3,262]{2,0,1:T(8,128)(2,1)S(1)}, u32[]{:S(2)}, u32[]{:S(2)}) %collective-permute-start.7) | collective-permute-done | bytes 150944 | tf_op jit(solution)/shard_map/ppermute | solution.py:14
  84.8 8.7 %fusion.223 = (f32[8,256]{1,0:T(8,128)S(1)}, f32[96,8,256]{2,0,1:T(8,128)S(1)}) fusion(bf16[96,11,262]{2,0,1:T(8,128)(2,1)S(1)} %get-tuple-element.165, f32[96]{0:T(128)} %get-tuple-element.217, f32[96]{0:T(128)} %get-tuple-element.218, f32[96]{0:T(128)S(1)} %get-tuple-element.171, f32[96]{0:T(128)S(1)} %get-tuple-element.172, ...), kind=kLoop, calls=%fused_computation.474 | loop fusion | flops 32438272 | bytes 17730944 | tf_op jit(solution)/shard_map/reduce_sum | solution.py:94
  94.5 1.9 convert_reduce_fusion
  96.4 1.0 multiply_reduce_fusion
  97.4 3.5 fusion.206
  100.9 1.1 fusion.138
  102.4 3.3 fusion.156
  106.0 17.7 %fusion.93 = f32[96,14,262]{2,0,1:T(8,128)S(1)} fusion(f32[96,8,256]{2,0,1:T(8,128)S(1)} %get-tuple-element.155, f32[96]{0:T(128)} %get-tuple-element.217, f32[96]{0:T(128)} %get-tuple-element.218, f32[96]{0:T(128)S(1)} %get-tuple-element.171, f32[96]{0:T(128)S(1)} %get-tuple-element.172, f32[96]{0:T(128)S(1)} %get-tuple-element.173, ...), kind=kLoop, calls=%fused_computation.144 | loop fusion | flops 34156416 | bytes 2213760 | tf_op jit(solution)/shard_map/add | solution.py:64
  124.5 1.0 copy.41
  125.5 2.6 fusion.188
  128.1 4.3 stack.199
  132.5 4.3 collective-permute-start.9
  136.7 2.8 convolution_bitcast_fusion.2
  139.6 2.8 collective-permute-start.10
  142.4 1.1 convolution_bitcast_fusion.3
  143.5 103.7 %all-reduce.1 = (f32[96,7,7]{0,2,1:T(8,128)S(1)}, f32[96]{0:T(128)S(1)}, f32[192]{0:T(256)S(1)}) all-reduce(f32[96,7,7]{0,2,1:T(8,128)S(1)} %reshape.198, f32[96]{0:T(128)S(1)} %copy-done.87, f32[192]{0:T(256)S(1)} %copy-done.97), channel_id=1, replica_groups=mesh['lon'=32,'lat'=16] {'lon','lat'}, use_global_device_ids=true, to_apply=%region_53.54 | all-reduce | flops 4992 | bytes 39936 | tf_op jit(solution)/shard_map/psum | solution.py:137
  247.2 4.5 %collective-permute-start.11 = (bf16[96,3,262]{2,0,1:T(8,128)(2,1)S(1)}, bf16[96,3,262]{2,0,1:T(8,128)(2,1)S(1)}, u32[]{:S(2)}, u32[]{:S(2)}) collective-permute-start(bf16[96,3,262]{2,0,1:T(8,128)(2,1)S(1)} %collective-permute-done.10), channel_id=1, source_target_pairs={{0,64},{64,0},{16,80},{80,16},{32,96},{96,32},{48,112},{112,48},{1... | collective-permute-start | bytes 452744 | tf_op jit(solution)/shard_map/ppermute | solution.py:14
  252.3 4.4 collective-permute-done.11
  256.6 3.0 collective-permute-start.12
  260.2 10.0 %collective-permute-done.12 = bf16[96,3,262]{2,0,1:T(8,128)(2,1)S(1)} collective-permute-done((bf16[96,3,262]{2,0,1:T(8,128)(2,1)S(1)}, bf16[96,3,262]{2,0,1:T(8,128)(2,1)S(1)}, u32[]{:S(2)}, u32[]{:S(2)}) %collective-permute-start.12) | collective-permute-done | bytes 150944 | tf_op jit(solution)/shard_map/ppermute | solution.py:14
  270.2 4.3 collective-permute-start.13
  275.0 12.5 %collective-permute-done.13 = bf16[96,3,262]{2,0,1:T(8,128)(2,1)S(1)} collective-permute-done((bf16[96,3,262]{2,0,1:T(8,128)(2,1)S(1)}, bf16[96,3,262]{2,0,1:T(8,128)(2,1)S(1)}, u32[]{:S(2)}, u32[]{:S(2)}) %collective-permute-start.13) | collective-permute-done | bytes 150944 | tf_op jit(solution)/shard_map/ppermute | solution.py:14
  289.4 2.0 collective-permute-start.14
  291.4 1.3 collective-permute-start.15
  292.6 120.1 %all-reduce.5.cloned.1.call-done = (f32[96,192]{1,0:T(8,128)}, f32[192,96]{1,0:T(8,128)}) async-done(((f32[96,192]{1,0:T(8,128)}, f32[192,96]{1,0:T(8,128)}), (f32[96,192]{1,0:T(8,128)}, f32[192,96]{1,0:T(8,128)})) %all-reduce.5.cloned.1.call-update) | async-done | bytes 147472 | tf_op jit(solution)/shard_map/psum | solution.py:137
  412.7 1.5 broadcast_multiply_fusion.1
  414.4 1.0 fusion.209
  415.4 1.1 fusion.208
  417.2 3.7 collective-permute-start.16
  422.1 1.9 collective-permute-start.17
  425.0 5.2 %collective-permute-done.17 = f32[3,768]{1,0:T(4,128)S(1)} collective-permute-done((f32[3,768]{1,0:T(4,128)S(1)}, f32[3,768]{1,0:T(4,128)S(1)}, u32[]{:S(2)}, u32[]{:S(2)}) %collective-permute-start.17) | collective-permute-done | bytes 9248 | tf_op jit(solution)/shard_map/ppermute | solution.py:25
  431.0 6.0 %scatter-add.21 = f32[96,8,256]{2,0,1:T(8,128)S(1)} dynamic-update-slice(f32[96,8,256]{2,0,1:T(8,128)S(1)} %slice.989, f32[96,8,3]{2,0,1:T(8,128)S(1)} %slice_add_fusion.3, s32[]{:T(128)} %constant.159.clone.1, s32[]{:T(128)} %constant.159.clone.1, s32[]{:T(128)} %constant.159.clone.1) | dynamic-update-slice | bytes 18436 | tf_op jit(solution)/shard_map/scatter-add | solution.py:155
  437.2 5.3 %scatter-add.24 = f32[96,8,256]{2,0,1:T(8,128)S(1)} dynamic-update-slice(f32[96,8,256]{2,0,1:T(8,128)S(1)} %scatter-add.21, f32[96,8,3]{2,0,1:T(8,128)S(1)} %slice_add_fusion.2, s32[]{:T(128)} %constant.159.clone.1, s32[]{:T(128)} %constant.159.clone.1, s32[]{:T(128)} %constant.173.clone.1) | dynamic-update-slice | bytes 18436 | tf_op jit(solution)/shard_map/scatter-add | solution.py:156
  (254 shorter events, 14.6 us)
Async XLA Ops:
  7.2 86.5 %copy-start = (bf16[96,192]{1,0:T(8,128)(2,1)S(1)}, bf16[96,192]{1,0:T(8,128)(2,1)}, u32[]{:S(2)}) copy-start(bf16[96,192]{1,0:T(8,128)(2,1)} %param.22) | copy-start | bytes 110596
  7.2 405.5 %all-reduce.5.cloned.1.call-start = ((), (), s32[]{:S(2)}) async-start(), calls=%async_computation | async-start | bytes 393216 | tf_op jit(solution)/shard_map/psum | solution.py:137
  9.1 8.9 %collective-permute-start = (bf16[96,8,3]{2,0,1:T(8,128)(2,1)S(1)}, bf16[96,8,3]{2,0,1:T(8,128)(2,1)S(1)}, u32[]{:S(2)}, u32[]{:S(2)}) collective-permute-start(bf16[96,8,3]{2,0,1:T(8,128)(2,1)S(1)} %get-tuple-element.168), channel_id=1, source_target_pairs={{0,16},{16,32},{32,48},{48,64},{64,80},{80,96},{96,112},{112,128},... | collective-permute-start | bytes 13832 | tf_op jit(solution)/shard_map/ppermute | solution.py:24
  15.4 12.2 %collective-permute-start.1 = (bf16[96,8,3]{2,0,1:T(8,128)(2,1)S(1)}, bf16[96,8,3]{2,0,1:T(8,128)(2,1)S(1)}, u32[]{:S(2)}, u32[]{:S(2)}) collective-permute-start(bf16[96,8,3]{2,0,1:T(8,128)(2,1)S(1)} %get-tuple-element.169), channel_id=1, source_target_pairs={{16,0},{32,16},{48,32},{64,48},{80,64},{96,80},{112,96},{128,112},... | collective-permute-start | bytes 13832 | tf_op jit(solution)/shard_map/ppermute | solution.py:25
  27.6 56.8 %copy-start.1 = (bf16[96,8,3]{2,0,1:T(8,128)(2,1)}, bf16[96,8,3]{2,0,1:T(8,128)(2,1)S(1)}, u32[]{:S(2)}) copy-start(bf16[96,8,3]{2,0,1:T(8,128)(2,1)S(1)} %collective-permute-done.1) | copy-start | bytes 13828
  27.9 3.4 collective-permute-start.3
  31.3 8.8 %collective-permute-start.4 = (bf16[96,3,262]{2,0,1:T(8,128)(2,1)S(1)}, bf16[96,3,262]{2,0,1:T(8,128)(2,1)S(1)}, u32[]{:S(2)}, u32[]{:S(2)}) collective-permute-start(bf16[96,3,262]{2,0,1:T(8,128)(2,1)S(1)} %collective-permute-done.3), channel_id=1, source_target_pairs={{0,32},{32,0},{16,48},{48,16},{64,96},{96,64},{80,112},{112,80},{1... | collective-permute-start | bytes 452744 | tf_op jit(solution)/shard_map/ppermute | solution.py:14
  33.2 51.2 %copy-start.11 = (f32[96]{0:T(128)}, f32[96]{0:T(128)S(1)}, u32[]{:S(2)}) copy-start(f32[96]{0:T(128)S(1)} %get-tuple-element.176) | copy-start | bytes 1156
  33.2 51.2 %copy-start.13 = (f32[96]{0:T(128)}, f32[96]{0:T(128)S(1)}, u32[]{:S(2)}) copy-start(f32[96]{0:T(128)S(1)} %get-tuple-element.177) | copy-start | bytes 1156
  33.2 51.2 %copy-start.15 = (f32[96]{0:T(128)}, f32[96]{0:T(128)S(1)}, u32[]{:S(2)}) copy-start(f32[96]{0:T(128)S(1)} %get-tuple-element.178) | copy-start | bytes 1156
  33.3 51.2 %copy-start.17 = (f32[96]{0:T(128)}, f32[96]{0:T(128)S(1)}, u32[]{:S(2)}) copy-start(f32[96]{0:T(128)S(1)} %get-tuple-element.179) | copy-start | bytes 1156
  33.3 51.2 %copy-start.19 = (f32[96]{0:T(128)}, f32[96]{0:T(128)S(1)}, u32[]{:S(2)}) copy-start(f32[96]{0:T(128)S(1)} %get-tuple-element.180) | copy-start | bytes 1156
  33.3 51.2 %copy-start.21 = (f32[96]{0:T(128)}, f32[96]{0:T(128)S(1)}, u32[]{:S(2)}) copy-start(f32[96]{0:T(128)S(1)} %get-tuple-element.181) | copy-start | bytes 1156
  33.3 51.2 %copy-start.23 = (f32[96]{0:T(128)}, f32[96]{0:T(128)S(1)}, u32[]{:S(2)}) copy-start(f32[96]{0:T(128)S(1)} %get-tuple-element.182) | copy-start | bytes 1156
  33.3 51.2 %copy-start.25 = (f32[96]{0:T(128)}, f32[96]{0:T(128)S(1)}, u32[]{:S(2)}) copy-start(f32[96]{0:T(128)S(1)} %get-tuple-element.183) | copy-start | bytes 1156
  33.3 51.2 %copy-start.27 = (f32[96]{0:T(128)}, f32[96]{0:T(128)S(1)}, u32[]{:S(2)}) copy-start(f32[96]{0:T(128)S(1)} %get-tuple-element.184) | copy-start | bytes 1156
  33.3 51.2 %copy-start.29 = (f32[96]{0:T(128)}, f32[96]{0:T(128)S(1)}, u32[]{:S(2)}) copy-start(f32[96]{0:T(128)S(1)} %get-tuple-element.185) | copy-start | bytes 1156
  33.3 51.2 %copy-start.31 = (f32[96]{0:T(128)}, f32[96]{0:T(128)S(1)}, u32[]{:S(2)}) copy-start(f32[96]{0:T(128)S(1)} %get-tuple-element.186) | copy-start | bytes 1156
  33.3 51.2 %copy-start.33 = (f32[96]{0:T(128)}, f32[96]{0:T(128)S(1)}, u32[]{:S(2)}) copy-start(f32[96]{0:T(128)S(1)} %get-tuple-element.187) | copy-start | bytes 1156
  33.3 51.2 %copy-start.35 = (f32[96]{0:T(128)}, f32[96]{0:T(128)S(1)}, u32[]{:S(2)}) copy-start(f32[96]{0:T(128)S(1)} %get-tuple-element.188) | copy-start | bytes 1156
  40.1 9.4 %collective-permute-start.5 = (bf16[96,3,262]{2,0,1:T(8,128)(2,1)S(1)}, bf16[96,3,262]{2,0,1:T(8,128)(2,1)S(1)}, u32[]{:S(2)}, u32[]{:S(2)}) collective-permute-start(bf16[96,3,262]{2,0,1:T(8,128)(2,1)S(1)} %collective-permute-done.4), channel_id=1, source_target_pairs={{0,64},{64,0},{16,80},{80,16},{32,96},{96,32},{48,112},{112,48},{1... | collective-permute-start | bytes 452744 | tf_op jit(solution)/shard_map/ppermute | solution.py:14
  44.2 40.3 %copy-start.37 = (f32[96]{0:T(128)}, f32[96]{0:T(128)S(1)}, u32[]{:S(2)}) copy-start(f32[96]{0:T(128)S(1)} %get-tuple-element.189) | copy-start | bytes 1156
  44.2 40.3 %copy-start.39 = (f32[96]{0:T(128)}, f32[96]{0:T(128)S(1)}, u32[]{:S(2)}) copy-start(f32[96]{0:T(128)S(1)} %get-tuple-element.190) | copy-start | bytes 1156
  44.2 40.3 %copy-start.41 = (f32[96]{0:T(128)}, f32[96]{0:T(128)S(1)}, u32[]{:S(2)}) copy-start(f32[96]{0:T(128)S(1)} %get-tuple-element.191) | copy-start | bytes 1156
  44.3 40.3 %copy-start.43 = (f32[96]{0:T(128)}, f32[96]{0:T(128)S(1)}, u32[]{:S(2)}) copy-start(f32[96]{0:T(128)S(1)} %get-tuple-element.192) | copy-start | bytes 1156
  44.3 40.3 %copy-start.45 = (f32[96]{0:T(128)}, f32[96]{0:T(128)S(1)}, u32[]{:S(2)}) copy-start(f32[96]{0:T(128)S(1)} %get-tuple-element.193) | copy-start | bytes 1156
  44.3 40.3 %copy-start.47 = (f32[96]{0:T(128)}, f32[96]{0:T(128)S(1)}, u32[]{:S(2)}) copy-start(f32[96]{0:T(128)S(1)} %get-tuple-element.194) | copy-start | bytes 1156
  44.3 40.3 %copy-start.49 = (f32[96]{0:T(128)}, f32[96]{0:T(128)S(1)}, u32[]{:S(2)}) copy-start(f32[96]{0:T(128)S(1)} %get-tuple-element.195) | copy-start | bytes 1156
  44.3 40.3 %copy-start.51 = (f32[96]{0:T(128)}, f32[96]{0:T(128)S(1)}, u32[]{:S(2)}) copy-start(f32[96]{0:T(128)S(1)} %get-tuple-element.196) | copy-start | bytes 1156
  44.3 40.3 %copy-start.53 = (f32[96]{0:T(128)}, f32[96]{0:T(128)S(1)}, u32[]{:S(2)}) copy-start(f32[96]{0:T(128)S(1)} %get-tuple-element.197) | copy-start | bytes 1156
  44.3 40.3 %copy-start.55 = (f32[96]{0:T(128)}, f32[96]{0:T(128)S(1)}, u32[]{:S(2)}) copy-start(f32[96]{0:T(128)S(1)} %get-tuple-element.198) | copy-start | bytes 1156
  44.3 40.3 %copy-start.57 = (f32[96]{0:T(128)}, f32[96]{0:T(128)S(1)}, u32[]{:S(2)}) copy-start(f32[96]{0:T(128)S(1)} %get-tuple-element.199) | copy-start | bytes 1156
  44.3 40.3 %copy-start.59 = (f32[96]{0:T(128)}, f32[96]{0:T(128)S(1)}, u32[]{:S(2)}) copy-start(f32[96]{0:T(128)S(1)} %get-tuple-element.200) | copy-start | bytes 1156
  44.3 40.3 %copy-start.61 = (f32[96]{0:T(128)}, f32[96]{0:T(128)S(1)}, u32[]{:S(2)}) copy-start(f32[96]{0:T(128)S(1)} %get-tuple-element.201) | copy-start | bytes 1156
  44.4 40.3 %copy-start.63 = (f32[96]{0:T(128)}, f32[96]{0:T(128)S(1)}, u32[]{:S(2)}) copy-start(f32[96]{0:T(128)S(1)} %get-tuple-element.202) | copy-start | bytes 1156
  44.4 28.5 %collective-permute-start.2 = (bf16[96,3,262]{2,0,1:T(8,128)(2,1)S(1)}, bf16[96,3,262]{2,0,1:T(8,128)(2,1)S(1)}, u32[]{:S(2)}, u32[]{:S(2)}) collective-permute-start(bf16[96,3,262]{2,0,1:T(8,128)(2,1)S(1)} %get-tuple-element.167), channel_id=1, source_target_pairs={{0,1},{1,2},{2,3},{3,4},{4,5},{5,6},{6,7},{7,8},{8,9},{9,10},{10,1... | collective-permute-start | bytes 452744 | tf_op jit(solution)/shard_map/ppermute | solution.py:24
  49.4 17.9 %collective-permute-start.6 = (bf16[96,3,262]{2,0,1:T(8,128)(2,1)S(1)}, bf16[96,3,262]{2,0,1:T(8,128)(2,1)S(1)}, u32[]{:S(2)}, u32[]{:S(2)}) collective-permute-start(bf16[96,3,262]{2,0,1:T(8,128)(2,1)S(1)} %collective-permute-done.5), channel_id=1, source_target_pairs={{0,128},{128,0},{16,144},{144,16},{32,160},{160,32},{48,176},{176,... | collective-permute-start | bytes 452744 | tf_op jit(solution)/shard_map/ppermute | solution.py:14
  58.1 25.6 %collective-permute-start.8 = (bf16[96,3,262]{2,0,1:T(8,128)(2,1)S(1)}, bf16[96,3,262]{2,0,1:T(8,128)(2,1)S(1)}, u32[]{:S(2)}, u32[]{:S(2)}) collective-permute-start(bf16[96,3,262]{2,0,1:T(8,128)(2,1)S(1)} %get-tuple-element.166), channel_id=1, source_target_pairs={{1,0},{2,1},{3,2},{4,3},{5,4},{6,5},{7,6},{8,7},{9,8},{10,9},{11,1... | collective-permute-start | bytes 452744 | tf_op jit(solution)/shard_map/ppermute | solution.py:25
  67.3 15.5 %collective-permute-start.7 = (bf16[96,3,262]{2,0,1:T(8,128)(2,1)S(1)}, bf16[96,3,262]{2,0,1:T(8,128)(2,1)S(1)}, u32[]{:S(2)}, u32[]{:S(2)}) collective-permute-start(bf16[96,3,262]{2,0,1:T(8,128)(2,1)S(1)} %collective-permute-done.6), channel_id=1, source_target_pairs={{0,256},{256,0},{16,272},{272,16},{32,288},{288,32},{48,304},{304,... | collective-permute-start | bytes 452744 | tf_op jit(solution)/shard_map/ppermute | solution.py:14
  132.5 7.1 %collective-permute-start.9 = (bf16[96,3,262]{2,0,1:T(8,128)(2,1)S(1)}, bf16[96,3,262]{2,0,1:T(8,128)(2,1)}, u32[]{:S(2)}, u32[]{:S(2)}) collective-permute-start(bf16[96,3,262]{2,0,1:T(8,128)(2,1)S(1)} %slice.1622), channel_id=1, source_target_pairs={{0,16},{16,0},{32,48},{48,32},{64,80},{80,64},{96,112},{112,96},{1... | collective-permute-start | bytes 452744 | tf_op jit(solution)/shard_map/ppermute | solution.py:14
  139.6 107.6 %collective-permute-start.10 = (bf16[96,3,262]{2,0,1:T(8,128)(2,1)}, bf16[96,3,262]{2,0,1:T(8,128)(2,1)S(1)}, u32[]{:S(2)}, u32[]{:S(2)}) collective-permute-start(bf16[96,3,262]{2,0,1:T(8,128)(2,1)} %collective-permute-done.9), channel_id=1, source_target_pairs={{0,32},{32,0},{16,48},{48,16},{64,96},{96,64},{80,112},{112,80},{1... | collective-permute-start | bytes 452744 | tf_op jit(solution)/shard_map/ppermute | solution.py:14
  247.2 9.5 %collective-permute-start.11 = (bf16[96,3,262]{2,0,1:T(8,128)(2,1)S(1)}, bf16[96,3,262]{2,0,1:T(8,128)(2,1)S(1)}, u32[]{:S(2)}, u32[]{:S(2)}) collective-permute-start(bf16[96,3,262]{2,0,1:T(8,128)(2,1)S(1)} %collective-permute-done.10), channel_id=1, source_target_pairs={{0,64},{64,0},{16,80},{80,16},{32,96},{96,32},{48,112},{112,48},{1... | collective-permute-start | bytes 452744 | tf_op jit(solution)/shard_map/ppermute | solution.py:14
  256.6 13.6 %collective-permute-start.12 = (bf16[96,3,262]{2,0,1:T(8,128)(2,1)S(1)}, bf16[96,3,262]{2,0,1:T(8,128)(2,1)S(1)}, u32[]{:S(2)}, u32[]{:S(2)}) collective-permute-start(bf16[96,3,262]{2,0,1:T(8,128)(2,1)S(1)} %collective-permute-done.11), channel_id=1, source_target_pairs={{0,128},{128,0},{16,144},{144,16},{32,160},{160,32},{48,176},{176,... | collective-permute-start | bytes 452744 | tf_op jit(solution)/shard_map/ppermute | solution.py:14
  270.2 17.3 %collective-permute-start.13 = (bf16[96,3,262]{2,0,1:T(8,128)(2,1)S(1)}, bf16[96,3,262]{2,0,1:T(8,128)(2,1)S(1)}, u32[]{:S(2)}, u32[]{:S(2)}) collective-permute-start(bf16[96,3,262]{2,0,1:T(8,128)(2,1)S(1)} %collective-permute-done.12), channel_id=1, source_target_pairs={{0,256},{256,0},{16,272},{272,16},{32,288},{288,32},{48,304},{304,... | collective-permute-start | bytes 452744 | tf_op jit(solution)/shard_map/ppermute | solution.py:14
  289.4 125.0 %collective-permute-start.14 = (bf16[96,3,262]{2,0,1:T(8,128)(2,1)S(1)}, bf16[96,3,262]{2,0,1:T(8,128)(2,1)}, u32[]{:S(2)}, u32[]{:S(2)}) collective-permute-start(bf16[96,3,262]{2,0,1:T(8,128)(2,1)S(1)} %get-tuple-element.162), channel_id=1, source_target_pairs={{0,1},{1,2},{2,3},{3,4},{4,5},{5,6},{6,7},{7,8},{8,9},{9,10},{10,1... | collective-permute-start | bytes 452744 | tf_op jit(solution)/shard_map/ppermute | solution.py:24
  291.4 123.0 %collective-permute-start.15 = (bf16[96,3,262]{2,0,1:T(8,128)(2,1)}, bf16[96,3,262]{2,0,1:T(8,128)(2,1)}, u32[]{:S(2)}, u32[]{:S(2)}) collective-permute-start(bf16[96,3,262]{2,0,1:T(8,128)(2,1)} %get-tuple-element.163), channel_id=1, source_target_pairs={{1,0},{2,1},{3,2},{4,3},{5,4},{6,5},{7,6},{8,7},{9,8},{10,9},{11,1... | collective-permute-start | bytes 452744 | tf_op jit(solution)/shard_map/ppermute | solution.py:25
  417.2 6.8 %collective-permute-start.16 = (f32[3,768]{1,0:T(4,128)S(1)}, f32[3,768]{1,0:T(4,128)S(1)}, u32[]{:S(2)}, u32[]{:S(2)}) collective-permute-start(f32[3,768]{1,0:T(4,128)S(1)} %slice.926), channel_id=1, source_target_pairs={{0,16},{16,32},{32,48},{48,64},{64,80},{80,96},{96,112},{112,128},... | collective-permute-start | bytes 27656 | tf_op jit(solution)/shard_map/ppermute | solution.py:24
  422.1 8.2 %collective-permute-start.17 = (f32[3,768]{1,0:T(4,128)S(1)}, f32[3,768]{1,0:T(4,128)S(1)}, u32[]{:S(2)}, u32[]{:S(2)}) collective-permute-start(f32[3,768]{1,0:T(4,128)S(1)} %slice.929), channel_id=1, source_target_pairs={{16,0},{32,16},{48,32},{64,48},{80,64},{96,80},{112,96},{128,112},... | collective-permute-start | bytes 27656 | tf_op jit(solution)/shard_map/ppermute | solution.py:25
  (70 other events, 660.9 us)
Sparse Core Ops, SparseCore 0:
  143.6 269.0 all-reduce.4
where the time goes:
time: 451 us
  waiting for transfers between devices  188 us (42%)
  blocking collectives  104 us (23%)
  starting transfers between devices  64.7 us (14%)
  other arithmetic  46.5 us (10%)
  local copies, waits for them, and re-layouts  24.3 us (5%)
  between operations  15.9 us (4%)
  matrix products  7.92 us (2%)
    psum x1, waiting for transfers between devices, shards(): lax.psum((kernel_part, gain_part, w_in_part, b_part, w_out_part), ('lon',...  120 us
    psum x1, blocking collectives, shards(): lax.psum((kernel_part, gain_part, w_in_part, b_part, w_out_part), ('lon',...  104 us
    ppermute x10, waiting for transfers between devices, from_partner(): return lax.ppermute(block, axis, route)  51.9 us
    ppermute x10, starting transfers between devices, from_partner(): return lax.ppermute(block, axis, route)  40.5 us
    add x1, other arithmetic, spread_back(): summed = summed + kernel[:, row_off, col_off][:, None, None] * window  17.7 us
    ppermute x4, waiting for transfers between devices, extended(): after = lax.ppermute(first, axis, down)  14.8 us
    ppermute x4, starting transfers between devices, extended(): before = lax.ppermute(last, axis, up)  13.9 us
    reduce_sum x4, other arithmetic, kernel_terms(): terms.append(jnp.sum(conv_grad * window, axis=(1, 2)))  10.5 us
  transfers between devices with their start and end apart: 19, of which 12 were waited for; matrix products, arithmetic and copies ran while one was open for 3% of the time, Pallas kernels for 0%

commit v1 on v0

--- a/solution.py
+++ b/solution.py
@@ -134,8 +134,14 @@
         b_part,
         ext_grad,
     )
-    kernel_sum, gain_sum, w_in_sum, b_sum, w_out_sum = lax.psum(
-        (kernel_part, gain_part, w_in_part, b_part, w_out_part), ("lon", "lat")
+
+    def _step_on_bands(payload, ax_name, group_axis):
+        x_new = lax.psum(payload, ax_name)
+        out_arr = lax.psum(x_new, group_axis)
+        return out_arr
+
+    kernel_sum, gain_sum, w_in_sum, b_sum, w_out_sum = _step_on_bands(
+        (kernel_part, gain_part, w_in_part, b_part, w_out_part), "lon", "lat"
     )
     returned = mirror_backward(ext_grad[:, tile_rows + 3 :, :])
     ext_grad = ext_grad.at[:, tile_rows : tile_rows + 3, :].add(

time: 451 us -> 607 us (1.35)
  blocking collectives: 104 us -> 170 us
  waiting for transfers between devices: 188 us -> 244 us
  starting transfers between devices: 64.7 us -> 97.2 us
    psum x1 -> x2, waiting for transfers between devices: 120 us -> 198 us  [the longest x1 136 us: _step_on_bands(): out_arr = lax.psum(x_new, group_axis)]
    psum x1 -> x2, blocking collectives: 104 us -> 170 us  [the longest x1 118 us: _step_on_bands(): x_new = lax.psum(payload, ax_name)]
    ppermute x10, waiting for transfers between devices: 51.9 us -> 30.7 us  [from_partner(): return lax.ppermute(block, axis, route)]
    ppermute x10, starting transfers between devices: 40.5 us -> 59.8 us  [from_partner(): return lax.ppermute(block, axis, route)]
    ppermute x4, starting transfers between devices: 13.9 us -> 27.1 us  [extended(): before = lax.ppermute(last, axis, up)]
  transfers between devices with their start and end apart: 19 -> 20, of which waited for: 12 -> 12; matrix products, arithmetic and copies ran while one was open for 3% -> 2% of each run, Pallas kernels for 0% -> 0%
where the time goes in v1:
time: 607 us; the launch traced here: 606 us
  waiting for transfers between devices  244 us (40%)
  blocking collectives  170 us (28%)
  starting transfers between devices  97.2 us (16%)
  other arithmetic  46.5 us (8%)
  local copies, waits for them, and re-layouts  24.3 us (4%)
  between operations  15.9 us (3%)
  matrix products  7.92 us (1%)
    psum x1, waiting for transfers between devices, _step_on_bands(): out_arr = lax.psum(x_new, group_axis)  136 us
    psum x1, blocking collectives, _step_on_bands(): x_new = lax.psum(payload, ax_name)  118 us
    psum x1, waiting for transfers between devices, _step_on_bands(): x_new = lax.psum(payload, ax_name)  61.8 us
    ppermute x10, starting transfers between devices, from_partner(): return lax.ppermute(block, axis, route)  59.8 us
    psum x1, blocking collectives, _step_on_bands(): out_arr = lax.psum(x_new, group_axis)  51.6 us
    ppermute x10, waiting for transfers between devices, from_partner(): return lax.ppermute(block, axis, route)  30.7 us
    ppermute x4, starting transfers between devices, extended(): before = lax.ppermute(last, axis, up)  27.1 us
    add x1, other arithmetic, spread_back(): summed = summed + kernel[:, row_off, col_off][:, None, None] * window  17.7 us
  transfers between devices with their start and end apart: 20, of which 12 were waited for; matrix products, arithmetic and copies ran while one was open for 2% of the time, Pallas kernels for 0%

profile of v1, /device:TPU:7, one launch (start us, length us, event | category | flops | bytes accessed | tf_op | source)
XLA Modules:
  0.0 605.7 jit_solution(9326804059304566500)
XLA Ops:
  7.9 1.1 copy_multiply_fusion.1
  9.1 6.3 %collective-permute-start = (bf16[96,8,3]{2,0,1:T(8,128)(2,1)S(1)}, bf16[96,8,3]{2,0,1:T(8,128)(2,1)S(1)}, u32[]{:S(2)}, u32[]{:S(2)}) collective-permute-start(bf16[96,8,3]{2,0,1:T(8,128)(2,1)S(1)} %get-tuple-element.173), channel_id=1, source_target_pairs={{0,16},{16,32},{32,48},{48,64},{64,80},{80,96},{96,112},{112,128},... | collective-permute-start | bytes 13832 | tf_op jit(solution)/shard_map/ppermute | solution.py:24
  15.4 1.9 collective-permute-start.1
  18.0 9.6 %collective-permute-done.1 = bf16[96,8,3]{2,0,1:T(8,128)(2,1)S(1)} collective-permute-done((bf16[96,8,3]{2,0,1:T(8,128)(2,1)S(1)}, bf16[96,8,3]{2,0,1:T(8,128)(2,1)S(1)}, u32[]{:S(2)}, u32[]{:S(2)}) %collective-permute-start.1) | collective-permute-done | bytes 4640 | tf_op jit(solution)/shard_map/ppermute | solution.py:25
  27.9 1.9 collective-permute-start.3
  29.8 1.4 collective-permute-done.3
  31.3 1.9 collective-permute-start.4
  33.4 6.7 %collective-permute-done.4 = bf16[96,3,262]{2,0,1:T(8,128)(2,1)S(1)} collective-permute-done((bf16[96,3,262]{2,0,1:T(8,128)(2,1)S(1)}, bf16[96,3,262]{2,0,1:T(8,128)(2,1)S(1)}, u32[]{:S(2)}, u32[]{:S(2)}) %collective-permute-start.4) | collective-permute-done | bytes 150944 | tf_op jit(solution)/shard_map/ppermute | solution.py:14
  40.1 4.1 collective-permute-start.5
  44.4 1.9 collective-permute-start.2
  46.3 3.1 collective-permute-done.5
  49.4 8.1 %collective-permute-start.6 = (bf16[96,3,262]{2,0,1:T(8,128)(2,1)S(1)}, bf16[96,3,262]{2,0,1:T(8,128)(2,1)S(1)}, u32[]{:S(2)}, u32[]{:S(2)}) collective-permute-start(bf16[96,3,262]{2,0,1:T(8,128)(2,1)S(1)} %collective-permute-done.5), channel_id=1, source_target_pairs={{0,128},{128,0},{16,144},{144,16},{32,160},{160,32},{48,176},{176,... | collective-permute-start | bytes 452744 | tf_op jit(solution)/shard_map/ppermute | solution.py:14
  58.1 5.2 collective-permute-start.8
  63.3 4.0 collective-permute-done.6
  67.3 5.6 collective-permute-start.7
  73.0 9.9 %collective-permute-done.7 = bf16[96,3,262]{2,0,1:T(8,128)(2,1)S(1)} collective-permute-done((bf16[96,3,262]{2,0,1:T(8,128)(2,1)S(1)}, bf16[96,3,262]{2,0,1:T(8,128)(2,1)S(1)}, u32[]{:S(2)}, u32[]{:S(2)}) %collective-permute-start.7) | collective-permute-done | bytes 150944 | tf_op jit(solution)/shard_map/ppermute | solution.py:14
  84.8 8.7 %fusion.223 = (f32[8,256]{1,0:T(8,128)S(1)}, f32[96,8,256]{2,0,1:T(8,128)S(1)}) fusion(bf16[96,11,262]{2,0,1:T(8,128)(2,1)S(1)} %get-tuple-element.170, f32[96]{0:T(128)} %get-tuple-element.222, f32[96]{0:T(128)} %get-tuple-element.223, f32[96]{0:T(128)S(1)} %get-tuple-element.176, f32[96]{0:T(128)S(1)} %get-tuple-element.177, ...), kind=kLoop, calls=%fused_computation.474 | loop fusion | flops 32438272 | bytes 17730944 | tf_op jit(solution)/shard_map/reduce_sum | solution.py:94
  94.5 1.9 convert_reduce_fusion
  96.4 1.0 multiply_reduce_fusion
  97.4 3.5 fusion.206
  100.9 1.1 fusion.138
  102.4 3.3 fusion.156
  106.0 17.7 %fusion.93 = f32[96,14,262]{2,0,1:T(8,128)S(1)} fusion(f32[96,8,256]{2,0,1:T(8,128)S(1)} %get-tuple-element.160, f32[96]{0:T(128)} %get-tuple-element.222, f32[96]{0:T(128)} %get-tuple-element.223, f32[96]{0:T(128)S(1)} %get-tuple-element.176, f32[96]{0:T(128)S(1)} %get-tuple-element.177, f32[96]{0:T(128)S(1)} %get-tuple-element.178, ...), kind=kLoop, calls=%fused_computation.144 | loop fusion | flops 34156416 | bytes 2213760 | tf_op jit(solution)/shard_map/add | solution.py:64
  125.5 2.6 fusion.188
  128.1 4.3 stack.199
  132.5 4.3 collective-permute-start.9
  136.7 2.8 convolution_bitcast_fusion.2
  139.6 2.8 collective-permute-start.10
  142.4 1.1 convolution_bitcast_fusion.3
  143.5 118.3 %all-reduce.1 = (f32[96,7,7]{0,2,1:T(8,128)S(1)}, f32[96]{0:T(128)S(1)}, f32[192]{0:T(256)S(1)}) all-reduce(f32[96,7,7]{0,2,1:T(8,128)S(1)} %reshape.198, f32[96]{0:T(128)S(1)} %copy-done.87, f32[192]{0:T(256)S(1)} %copy-done.97), channel_id=1, replica_groups=mesh['lon'=32,'lat'=16] {'lon'}, use_global_device_ids=true, to_apply=%region_53.54 | all-reduce | flops 4992 | bytes 39936 | tf_op jit(solution)/shard_map/psum | solution.py:139
  261.8 51.6 %all-reduce.3 = (f32[96,7,7]{0,2,1:T(8,128)S(1)}, f32[96]{0:T(128)S(1)}, f32[192]{0:T(256)S(1)}) all-reduce(f32[96,7,7]{0,2,1:T(8,128)S(1)} %get-tuple-element.150, f32[96]{0:T(128)S(1)} %get-tuple-element.151, f32[192]{0:T(256)S(1)} %get-tuple-element.152), channel_id=1, replica_groups=mesh['lon'=32,'lat'=16] {'lat'}, use_global_device_ids=true, to_apply=%region_54.55 | all-reduce | flops 4992 | bytes 39936 | tf_op jit(solution)/shard_map/psum | solution.py:140
  313.4 13.8 %collective-permute-start.11 = (bf16[96,3,262]{2,0,1:T(8,128)(2,1)S(1)}, bf16[96,3,262]{2,0,1:T(8,128)(2,1)S(1)}, u32[]{:S(2)}, u32[]{:S(2)}) collective-permute-start(bf16[96,3,262]{2,0,1:T(8,128)(2,1)S(1)} %collective-permute-done.10), channel_id=1, source_target_pairs={{0,64},{64,0},{16,80},{80,16},{32,96},{96,32},{48,112},{112,48},{1... | collective-permute-start | bytes 452744 | tf_op jit(solution)/shard_map/ppermute | solution.py:14
  327.8 2.7 collective-permute-done.11
  330.5 14.3 %collective-permute-start.12 = (bf16[96,3,262]{2,0,1:T(8,128)(2,1)S(1)}, bf16[96,3,262]{2,0,1:T(8,128)(2,1)S(1)}, u32[]{:S(2)}, u32[]{:S(2)}) collective-permute-start(bf16[96,3,262]{2,0,1:T(8,128)(2,1)S(1)} %collective-permute-done.11), channel_id=1, source_target_pairs={{0,128},{128,0},{16,144},{144,16},{32,160},{160,32},{48,176},{176,... | collective-permute-start | bytes 452744 | tf_op jit(solution)/shard_map/ppermute | solution.py:14
  345.4 2.8 collective-permute-done.12
  348.2 3.0 collective-permute-start.13
  351.7 61.8 %all-reduce.8.cloned.1.call-done = (f32[96,192]{1,0:T(8,128)}, f32[192,96]{1,0:T(8,128)}) async-done(((f32[96,192]{1,0:T(8,128)}, f32[192,96]{1,0:T(8,128)}), (f32[96,192]{1,0:T(8,128)}, f32[192,96]{1,0:T(8,128)})) %all-reduce.8.cloned.1.call-update) | async-done | bytes 147472 | tf_op jit(solution)/shard_map/psum | solution.py:139
  415.5 3.1 collective-permute-start.14
  418.6 1.3 collective-permute-start.15
  419.8 136.0 %all-reduce.10.cloned.1.call-done = (f32[96,192]{1,0:T(8,128)}, f32[192,96]{1,0:T(8,128)}) async-done(((f32[96,192]{1,0:T(8,128)}, f32[192,96]{1,0:T(8,128)}), (f32[96,192]{1,0:T(8,128)}, f32[192,96]{1,0:T(8,128)})) %all-reduce.10.cloned.1.call-update) | async-done | bytes 147472 | tf_op jit(solution)/shard_map/psum | solution.py:140
  555.9 1.5 broadcast_multiply_fusion.1
  557.5 1.0 fusion.209
  558.5 1.1 fusion.208
  560.4 15.8 %collective-permute-start.16 = (f32[3,768]{1,0:T(4,128)S(1)}, f32[3,768]{1,0:T(4,128)S(1)}, u32[]{:S(2)}, u32[]{:S(2)}) collective-permute-start(f32[3,768]{1,0:T(4,128)S(1)} %slice.926), channel_id=1, source_target_pairs={{0,16},{16,32},{32,48},{48,64},{64,80},{80,96},{96,112},{112,128},... | collective-permute-start | bytes 27656 | tf_op jit(solution)/shard_map/ppermute | solution.py:24
  577.4 1.9 collective-permute-start.17
  580.3 5.1 collective-permute-done.17
  586.2 6.0 scatter-add.21
  592.4 5.3 scatter-add.24
  (258 shorter events, 15.6 us)
Async XLA Ops:
  7.2 86.5 %copy-start = (bf16[96,192]{1,0:T(8,128)(2,1)S(1)}, bf16[96,192]{1,0:T(8,128)(2,1)}, u32[]{:S(2)}) copy-start(bf16[96,192]{1,0:T(8,128)(2,1)} %param.22) | copy-start | bytes 110596
  7.2 406.4 %all-reduce.8.cloned.1.call-start = ((), (), s32[]{:S(2)}) async-start(), calls=%async_computation | async-start | bytes 393216 | tf_op jit(solution)/shard_map/psum | solution.py:139
  9.1 8.9 %collective-permute-start = (bf16[96,8,3]{2,0,1:T(8,128)(2,1)S(1)}, bf16[96,8,3]{2,0,1:T(8,128)(2,1)S(1)}, u32[]{:S(2)}, u32[]{:S(2)}) collective-permute-start(bf16[96,8,3]{2,0,1:T(8,128)(2,1)S(1)} %get-tuple-element.173), channel_id=1, source_target_pairs={{0,16},{16,32},{32,48},{48,64},{64,80},{80,96},{96,112},{112,128},... | collective-permute-start | bytes 13832 | tf_op jit(solution)/shard_map/ppermute | solution.py:24
  15.4 12.2 %collective-permute-start.1 = (bf16[96,8,3]{2,0,1:T(8,128)(2,1)S(1)}, bf16[96,8,3]{2,0,1:T(8,128)(2,1)S(1)}, u32[]{:S(2)}, u32[]{:S(2)}) collective-permute-start(bf16[96,8,3]{2,0,1:T(8,128)(2,1)S(1)} %get-tuple-element.174), channel_id=1, source_target_pairs={{16,0},{32,16},{48,32},{64,48},{80,64},{96,80},{112,96},{128,112},... | collective-permute-start | bytes 13832 | tf_op jit(solution)/shard_map/ppermute | solution.py:25
  27.6 56.8 %copy-start.1 = (bf16[96,8,3]{2,0,1:T(8,128)(2,1)}, bf16[96,8,3]{2,0,1:T(8,128)(2,1)S(1)}, u32[]{:S(2)}) copy-start(bf16[96,8,3]{2,0,1:T(8,128)(2,1)S(1)} %collective-permute-done.1) | copy-start | bytes 13828
  27.9 3.4 collective-permute-start.3
  31.3 8.8 %collective-permute-start.4 = (bf16[96,3,262]{2,0,1:T(8,128)(2,1)S(1)}, bf16[96,3,262]{2,0,1:T(8,128)(2,1)S(1)}, u32[]{:S(2)}, u32[]{:S(2)}) collective-permute-start(bf16[96,3,262]{2,0,1:T(8,128)(2,1)S(1)} %collective-permute-done.3), channel_id=1, source_target_pairs={{0,32},{32,0},{16,48},{48,16},{64,96},{96,64},{80,112},{112,80},{1... | collective-permute-start | bytes 452744 | tf_op jit(solution)/shard_map/ppermute | solution.py:14
  33.2 51.2 %copy-start.11 = (f32[96]{0:T(128)}, f32[96]{0:T(128)S(1)}, u32[]{:S(2)}) copy-start(f32[96]{0:T(128)S(1)} %get-tuple-element.181) | copy-start | bytes 1156
  33.2 51.2 %copy-start.13 = (f32[96]{0:T(128)}, f32[96]{0:T(128)S(1)}, u32[]{:S(2)}) copy-start(f32[96]{0:T(128)S(1)} %get-tuple-element.182) | copy-start | bytes 1156
  33.2 51.2 %copy-start.15 = (f32[96]{0:T(128)}, f32[96]{0:T(128)S(1)}, u32[]{:S(2)}) copy-start(f32[96]{0:T(128)S(1)} %get-tuple-element.183) | copy-start | bytes 1156
  33.3 51.2 %copy-start.17 = (f32[96]{0:T(128)}, f32[96]{0:T(128)S(1)}, u32[]{:S(2)}) copy-start(f32[96]{0:T(128)S(1)} %get-tuple-element.184) | copy-start | bytes 1156
  33.3 51.2 %copy-start.19 = (f32[96]{0:T(128)}, f32[96]{0:T(128)S(1)}, u32[]{:S(2)}) copy-start(f32[96]{0:T(128)S(1)} %get-tuple-element.185) | copy-start | bytes 1156
  33.3 51.2 %copy-start.21 = (f32[96]{0:T(128)}, f32[96]{0:T(128)S(1)}, u32[]{:S(2)}) copy-start(f32[96]{0:T(128)S(1)} %get-tuple-element.186) | copy-start | bytes 1156
  33.3 51.2 %copy-start.23 = (f32[96]{0:T(128)}, f32[96]{0:T(128)S(1)}, u32[]{:S(2)}) copy-start(f32[96]{0:T(128)S(1)} %get-tuple-element.187) | copy-start | bytes 1156
  33.3 51.2 %copy-start.25 = (f32[96]{0:T(128)}, f32[96]{0:T(128)S(1)}, u32[]{:S(2)}) copy-start(f32[96]{0:T(128)S(1)} %get-tuple-element.188) | copy-start | bytes 1156
  33.3 51.2 %copy-start.27 = (f32[96]{0:T(128)}, f32[96]{0:T(128)S(1)}, u32[]{:S(2)}) copy-start(f32[96]{0:T(128)S(1)} %get-tuple-element.189) | copy-start | bytes 1156
  33.3 51.2 %copy-start.29 = (f32[96]{0:T(128)}, f32[96]{0:T(128)S(1)}, u32[]{:S(2)}) copy-start(f32[96]{0:T(128)S(1)} %get-tuple-element.190) | copy-start | bytes 1156
  33.3 51.2 %copy-start.31 = (f32[96]{0:T(128)}, f32[96]{0:T(128)S(1)}, u32[]{:S(2)}) copy-start(f32[96]{0:T(128)S(1)} %get-tuple-element.191) | copy-start | bytes 1156
  33.3 51.2 %copy-start.33 = (f32[96]{0:T(128)}, f32[96]{0:T(128)S(1)}, u32[]{:S(2)}) copy-start(f32[96]{0:T(128)S(1)} %get-tuple-element.192) | copy-start | bytes 1156
  33.3 51.2 %copy-start.35 = (f32[96]{0:T(128)}, f32[96]{0:T(128)S(1)}, u32[]{:S(2)}) copy-start(f32[96]{0:T(128)S(1)} %get-tuple-element.193) | copy-start | bytes 1156
  40.1 9.4 %collective-permute-start.5 = (bf16[96,3,262]{2,0,1:T(8,128)(2,1)S(1)}, bf16[96,3,262]{2,0,1:T(8,128)(2,1)S(1)}, u32[]{:S(2)}, u32[]{:S(2)}) collective-permute-start(bf16[96,3,262]{2,0,1:T(8,128)(2,1)S(1)} %collective-permute-done.4), channel_id=1, source_target_pairs={{0,64},{64,0},{16,80},{80,16},{32,96},{96,32},{48,112},{112,48},{1... | collective-permute-start | bytes 452744 | tf_op jit(solution)/shard_map/ppermute | solution.py:14
  44.2 40.3 %copy-start.37 = (f32[96]{0:T(128)}, f32[96]{0:T(128)S(1)}, u32[]{:S(2)}) copy-start(f32[96]{0:T(128)S(1)} %get-tuple-element.194) | copy-start | bytes 1156
  44.2 40.3 %copy-start.39 = (f32[96]{0:T(128)}, f32[96]{0:T(128)S(1)}, u32[]{:S(2)}) copy-start(f32[96]{0:T(128)S(1)} %get-tuple-element.195) | copy-start | bytes 1156
  44.2 40.3 %copy-start.41 = (f32[96]{0:T(128)}, f32[96]{0:T(128)S(1)}, u32[]{:S(2)}) copy-start(f32[96]{0:T(128)S(1)} %get-tuple-element.196) | copy-start | bytes 1156
  44.3 40.3 %copy-start.43 = (f32[96]{0:T(128)}, f32[96]{0:T(128)S(1)}, u32[]{:S(2)}) copy-start(f32[96]{0:T(128)S(1)} %get-tuple-element.197) | copy-start | bytes 1156
  44.3 40.3 %copy-start.45 = (f32[96]{0:T(128)}, f32[96]{0:T(128)S(1)}, u32[]{:S(2)}) copy-start(f32[96]{0:T(128)S(1)} %get-tuple-element.198) | copy-start | bytes 1156
  44.3 40.3 %copy-start.47 = (f32[96]{0:T(128)}, f32[96]{0:T(128)S(1)}, u32[]{:S(2)}) copy-start(f32[96]{0:T(128)S(1)} %get-tuple-element.199) | copy-start | bytes 1156
  44.3 40.3 %copy-start.49 = (f32[96]{0:T(128)}, f32[96]{0:T(128)S(1)}, u32[]{:S(2)}) copy-start(f32[96]{0:T(128)S(1)} %get-tuple-element.200) | copy-start | bytes 1156
  44.3 40.3 %copy-start.51 = (f32[96]{0:T(128)}, f32[96]{0:T(128)S(1)}, u32[]{:S(2)}) copy-start(f32[96]{0:T(128)S(1)} %get-tuple-element.201) | copy-start | bytes 1156
  44.3 40.3 %copy-start.53 = (f32[96]{0:T(128)}, f32[96]{0:T(128)S(1)}, u32[]{:S(2)}) copy-start(f32[96]{0:T(128)S(1)} %get-tuple-element.202) | copy-start | bytes 1156
  44.3 40.3 %copy-start.55 = (f32[96]{0:T(128)}, f32[96]{0:T(128)S(1)}, u32[]{:S(2)}) copy-start(f32[96]{0:T(128)S(1)} %get-tuple-element.203) | copy-start | bytes 1156
  44.3 40.3 %copy-start.57 = (f32[96]{0:T(128)}, f32[96]{0:T(128)S(1)}, u32[]{:S(2)}) copy-start(f32[96]{0:T(128)S(1)} %get-tuple-element.204) | copy-start | bytes 1156
  44.3 40.3 %copy-start.59 = (f32[96]{0:T(128)}, f32[96]{0:T(128)S(1)}, u32[]{:S(2)}) copy-start(f32[96]{0:T(128)S(1)} %get-tuple-element.205) | copy-start | bytes 1156
  44.3 40.3 %copy-start.61 = (f32[96]{0:T(128)}, f32[96]{0:T(128)S(1)}, u32[]{:S(2)}) copy-start(f32[96]{0:T(128)S(1)} %get-tuple-element.206) | copy-start | bytes 1156
  44.4 28.5 %collective-permute-start.2 = (bf16[96,3,262]{2,0,1:T(8,128)(2,1)S(1)}, bf16[96,3,262]{2,0,1:T(8,128)(2,1)S(1)}, u32[]{:S(2)}, u32[]{:S(2)}) collective-permute-start(bf16[96,3,262]{2,0,1:T(8,128)(2,1)S(1)} %get-tuple-element.172), channel_id=1, source_target_pairs={{0,1},{1,2},{2,3},{3,4},{4,5},{5,6},{6,7},{7,8},{8,9},{9,10},{10,1... | collective-permute-start | bytes 452744 | tf_op jit(solution)/shard_map/ppermute | solution.py:24
  49.4 17.9 %collective-permute-start.6 = (bf16[96,3,262]{2,0,1:T(8,128)(2,1)S(1)}, bf16[96,3,262]{2,0,1:T(8,128)(2,1)S(1)}, u32[]{:S(2)}, u32[]{:S(2)}) collective-permute-start(bf16[96,3,262]{2,0,1:T(8,128)(2,1)S(1)} %collective-permute-done.5), channel_id=1, source_target_pairs={{0,128},{128,0},{16,144},{144,16},{32,160},{160,32},{48,176},{176,... | collective-permute-start | bytes 452744 | tf_op jit(solution)/shard_map/ppermute | solution.py:14
  58.1 25.6 %collective-permute-start.8 = (bf16[96,3,262]{2,0,1:T(8,128)(2,1)S(1)}, bf16[96,3,262]{2,0,1:T(8,128)(2,1)S(1)}, u32[]{:S(2)}, u32[]{:S(2)}) collective-permute-start(bf16[96,3,262]{2,0,1:T(8,128)(2,1)S(1)} %get-tuple-element.171), channel_id=1, source_target_pairs={{1,0},{2,1},{3,2},{4,3},{5,4},{6,5},{7,6},{8,7},{9,8},{10,9},{11,1... | collective-permute-start | bytes 452744 | tf_op jit(solution)/shard_map/ppermute | solution.py:25
  67.3 15.5 %collective-permute-start.7 = (bf16[96,3,262]{2,0,1:T(8,128)(2,1)S(1)}, bf16[96,3,262]{2,0,1:T(8,128)(2,1)S(1)}, u32[]{:S(2)}, u32[]{:S(2)}) collective-permute-start(bf16[96,3,262]{2,0,1:T(8,128)(2,1)S(1)} %collective-permute-done.6), channel_id=1, source_target_pairs={{0,256},{256,0},{16,272},{272,16},{32,288},{288,32},{48,304},{304,... | collective-permute-start | bytes 452744 | tf_op jit(solution)/shard_map/ppermute | solution.py:14
  132.5 7.1 %collective-permute-start.9 = (bf16[96,3,262]{2,0,1:T(8,128)(2,1)S(1)}, bf16[96,3,262]{2,0,1:T(8,128)(2,1)}, u32[]{:S(2)}, u32[]{:S(2)}) collective-permute-start(bf16[96,3,262]{2,0,1:T(8,128)(2,1)S(1)} %slice.1622), channel_id=1, source_target_pairs={{0,16},{16,0},{32,48},{48,32},{64,80},{80,64},{96,112},{112,96},{1... | collective-permute-start | bytes 452744 | tf_op jit(solution)/shard_map/ppermute | solution.py:14
  139.6 173.8 %collective-permute-start.10 = (bf16[96,3,262]{2,0,1:T(8,128)(2,1)}, bf16[96,3,262]{2,0,1:T(8,128)(2,1)S(1)}, u32[]{:S(2)}, u32[]{:S(2)}) collective-permute-start(bf16[96,3,262]{2,0,1:T(8,128)(2,1)} %collective-permute-done.9), channel_id=1, source_target_pairs={{0,32},{32,0},{16,48},{48,16},{64,96},{96,64},{80,112},{112,80},{1... | collective-permute-start | bytes 452744 | tf_op jit(solution)/shard_map/ppermute | solution.py:14
  143.5 412.4 %all-reduce.10.cloned.1.call-start = ((), (), s32[]{:S(2)}) async-start(), calls=%async_computation.1 | async-start | bytes 393216 | tf_op jit(solution)/shard_map/psum | solution.py:140
  313.4 17.1 %collective-permute-start.11 = (bf16[96,3,262]{2,0,1:T(8,128)(2,1)S(1)}, bf16[96,3,262]{2,0,1:T(8,128)(2,1)S(1)}, u32[]{:S(2)}, u32[]{:S(2)}) collective-permute-start(bf16[96,3,262]{2,0,1:T(8,128)(2,1)S(1)} %collective-permute-done.10), channel_id=1, source_target_pairs={{0,64},{64,0},{16,80},{80,16},{32,96},{96,32},{48,112},{112,48},{1... | collective-permute-start | bytes 452744 | tf_op jit(solution)/shard_map/ppermute | solution.py:14
  330.5 17.7 %collective-permute-start.12 = (bf16[96,3,262]{2,0,1:T(8,128)(2,1)S(1)}, bf16[96,3,262]{2,0,1:T(8,128)(2,1)S(1)}, u32[]{:S(2)}, u32[]{:S(2)}) collective-permute-start(bf16[96,3,262]{2,0,1:T(8,128)(2,1)S(1)} %collective-permute-done.11), channel_id=1, source_target_pairs={{0,128},{128,0},{16,144},{144,16},{32,160},{160,32},{48,176},{176,... | collective-permute-start | bytes 452744 | tf_op jit(solution)/shard_map/ppermute | solution.py:14
  348.2 65.4 %collective-permute-start.13 = (bf16[96,3,262]{2,0,1:T(8,128)(2,1)S(1)}, bf16[96,3,262]{2,0,1:T(8,128)(2,1)S(1)}, u32[]{:S(2)}, u32[]{:S(2)}) collective-permute-start(bf16[96,3,262]{2,0,1:T(8,128)(2,1)S(1)} %collective-permute-done.12), channel_id=1, source_target_pairs={{0,256},{256,0},{16,272},{272,16},{32,288},{288,32},{48,304},{304,... | collective-permute-start | bytes 452744 | tf_op jit(solution)/shard_map/ppermute | solution.py:14
  415.5 142.0 %collective-permute-start.14 = (bf16[96,3,262]{2,0,1:T(8,128)(2,1)S(1)}, bf16[96,3,262]{2,0,1:T(8,128)(2,1)}, u32[]{:S(2)}, u32[]{:S(2)}) collective-permute-start(bf16[96,3,262]{2,0,1:T(8,128)(2,1)S(1)} %get-tuple-element.167), channel_id=1, source_target_pairs={{0,1},{1,2},{2,3},{3,4},{4,5},{5,6},{6,7},{7,8},{8,9},{9,10},{10,1... | collective-permute-start | bytes 452744 | tf_op jit(solution)/shard_map/ppermute | solution.py:24
  418.6 139.0 %collective-permute-start.15 = (bf16[96,3,262]{2,0,1:T(8,128)(2,1)}, bf16[96,3,262]{2,0,1:T(8,128)(2,1)}, u32[]{:S(2)}, u32[]{:S(2)}) collective-permute-start(bf16[96,3,262]{2,0,1:T(8,128)(2,1)} %get-tuple-element.168), channel_id=1, source_target_pairs={{1,0},{2,1},{3,2},{4,3},{5,4},{6,5},{7,6},{8,7},{9,8},{10,9},{11,1... | collective-permute-start | bytes 452744 | tf_op jit(solution)/shard_map/ppermute | solution.py:25
  560.4 18.9 %collective-permute-start.16 = (f32[3,768]{1,0:T(4,128)S(1)}, f32[3,768]{1,0:T(4,128)S(1)}, u32[]{:S(2)}, u32[]{:S(2)}) collective-permute-start(f32[3,768]{1,0:T(4,128)S(1)} %slice.926), channel_id=1, source_target_pairs={{0,16},{16,32},{32,48},{48,64},{64,80},{80,96},{96,112},{112,128},... | collective-permute-start | bytes 27656 | tf_op jit(solution)/shard_map/ppermute | solution.py:24
  577.4 8.0 %collective-permute-start.17 = (f32[3,768]{1,0:T(4,128)S(1)}, f32[3,768]{1,0:T(4,128)S(1)}, u32[]{:S(2)}, u32[]{:S(2)}) collective-permute-start(f32[3,768]{1,0:T(4,128)S(1)} %slice.929), channel_id=1, source_target_pairs={{16,0},{32,16},{48,32},{64,48},{80,64},{96,80},{112,96},{128,112},... | collective-permute-start | bytes 27656 | tf_op jit(solution)/shard_map/ppermute | solution.py:25
  (71 other events, 713.3 us)
Sparse Core Ops, SparseCore 0:
  143.6 269.9 all-reduce.7
  416.8 139.0 all-reduce.9
